TPU v7x, 32 devices: a whole 2x2x4 slice. The times are simulated.
32 devices in a mesh: parts: 2 (over y), wide: 16 (over z, x, core).
Axes of the slice: x: 2, y: 2, z: 4, core: 2. Of those that a mesh axis runs over, the one named last changes fastest.
Arguments:
- amplitudes: bfloat16 [2048, 262144], P(('parts', 'wide')), parts along dimension 0, may hold values from -6 to 6
- integrals: bfloat16 [2048, 262144], P('parts', 'wide'), parts along dimension 0, may hold values from -0.03125 to 0.03125
- occ_irrep: int32 [64], P('parts'), parts along dimension 0, may hold values from 0 to 7
- vir_irrep: int32 [16], P('parts'), parts along dimension 0, may hold values from 0 to 7, as said below
- occ_energy: float32 [64], P('parts'), parts along dimension 0, may hold values from -1.5 to -0.5
- vir_energy: float32 [1024], P('parts'), parts along dimension 0, may hold values from 0.5 to 2.5
Outputs:
- ladder: float32 [2048, 1024], P(('parts', 'wide')), parts along dimension 0
There are 2 independent parts, one for each index of `parts`. A program takes and returns all parts, laid end to end along the dimension named above; each array names one. Nothing has to cross between parts.
Inputs may be any that keep to these rules, and one draw needn't show every extreme that they name: `vir_irrep`: 6 of the blocks carry one common label, which lies between 1 and 6; of the other two blocks one carries label 0 and one label 7. Which blocks these are is arbitrary.
All inputs are finite; a program needn't handle non-finite values.
Results may differ from a plain program's by a relative error of at most 0.0003.
Values may be sent and summed in bfloat16 or wider, within the bound.
No kernel may reach another device: no remote copies, remote signals or barrier semaphores. Data moves between devices by JAX's collectives and lax.ppermute only.
A program may use at most 256 MiB of HBM per device.

v0:
```python
import jax
import jax.numpy as jnp
from jax import lax
from jax.sharding import PartitionSpec as P

BLK = 64


def block_lookup(table, block_ids):
    labels = jnp.arange(table.shape[0], dtype=jnp.int32)
    hits = block_ids[:, None] == labels[None, :]
    return jnp.sum(jnp.where(hits, table[None, :], 0), axis=1)


def contract(left, right):
    return lax.dot_general(
        left, right, (((1,), (1,)), ((), ())), preferred_element_type=jnp.float32
    )


def body(amplitudes, integrals, occ_irrep, vir_irrep, occ_energy, vir_energy):
    position = lax.axis_index("wide")
    pairs_local = amplitudes.shape[0]
    local_cols = integrals.shape[1]
    nvir = vir_energy.shape[0]
    slab_rows = integrals.shape[0]
    slab_first = slab_rows // nvir
    gathered = lax.all_to_all(amplitudes, "wide", split_axis=1, concat_axis=0, tiled=True)
    flat_cols = position * local_cols + jnp.arange(local_cols, dtype=jnp.int32)
    first_vir = flat_cols // nvir
    second_vir = flat_cols % nvir
    col_irrep = jnp.bitwise_xor(
        block_lookup(vir_irrep, first_vir // BLK), block_lookup(vir_irrep, second_vir // BLK)
    )
    vir_label = block_lookup(vir_irrep, jnp.arange(nvir, dtype=jnp.int32) // BLK)
    pair_irrep = jnp.bitwise_xor(occ_irrep[:, None], occ_irrep[None, :]).reshape(-1)
    slab_irrep = jnp.bitwise_xor(vir_label[:slab_first, None], vir_label[None, :]).reshape(-1)
    kept_t = jnp.where(pair_irrep[:, None] == col_irrep[None, :], gathered, 0)
    kept_v = jnp.where(slab_irrep[:, None] == col_irrep[None, :], integrals, 0)
    summed = lax.psum_scatter(contract(kept_t, kept_v), "wide", scatter_dimension=0, tiled=True)
    slab_energy = (vir_energy[:slab_first, None] + vir_energy[None, :]).reshape(-1)
    pair_energy = (occ_energy[:, None] + occ_energy[None, :]).reshape(-1)
    local_pair_energy = lax.dynamic_slice_in_dim(
        pair_energy, position * pairs_local, pairs_local, 0
    )
    denominator = slab_energy[None, :] - local_pair_energy[:, None]
    return summed / denominator


def solution(mesh):
    return jax.shard_map(
        body,
        mesh=mesh,
        in_specs=(
            P(("parts", "wide"), None),
            P("parts", "wide"),
            P("parts"),
            P("parts"),
            P("parts"),
            P("parts"),
        ),
        out_specs=P(("parts", "wide"), None),
        check_vma=False,
    )
```

profile of v0, /device:TPU:0, one launch (start us, length us, event | category | flops | bytes accessed | tf_op | source)
XLA Modules:
  0.0 883.8 jit_solution(14296305826773855284)
XLA Ops:
  6.5 22.8 %copy.13 = bf16[8,16,8,16384]{3,2,0,1:T(8,128)(2,1)} copy(bf16[8,16,8,16384]{3,2,1,0:T(8,128)(2,1)} %bitcast.14) | data formatting | bytes 67108864 | tf_op jit(solution)/shard_map/all_to_all | solution.py:28
  29.4 0.0 copy-start
  29.4 7.6 all-to-all-start
  36.9 0.0 reduce-scatter.2.cloned.1.call-start
  37.0 0.0 copy-done
  37.0 0.1 select_reduce_fusion.2
  37.1 0.1 xor_bitcast_fusion
  37.2 0.0 copy-done.1
  37.2 0.1 broadcast_xor_fusion
  37.3 0.1 xor.50
  37.3 0.1 add_select_fusion
  37.5 0.4 select_reduce_fusion
  37.9 587.9 %all-to-all-done = bf16[64,16,16384]{2,0,1:T(8,128)(2,1)} async-done(((bf16[64,16,16384]{2,0,1:T(8,128)(2,1)}), bf16[64,16,16384]{2,0,1:T(8,128)(2,1)}, u32[]{:S(2)}, u32[]{:S(2)}) %all-to-all-start) | async-done | bytes 33554464 | tf_op jit(solution)/shard_map/all_to_all | solution.py:28
  625.8 43.9 %fusion = f32[1024,1024]{1,0:T(8,128)} fusion(bf16[1024,16384]{1,0:T(8,128)(2,1)} %bitcast.1, bf16[1024,16384]{1,0:T(8,128)(2,1)} %param.7, s32[16384]{0:T(1024)S(1)} %xor.51, s32[1024]{0:T(1024)S(1)} %bitcast.16, s32[1024]{0:T(1024)S(1)} %xor.50), kind=kOutput, calls=%fused_computation.2 | convolution fusion | flops 34426847232 | bytes 71376896 | tf_op jit(solution)/shard_map/dot_general | solution.py:16
  669.7 0.0 reduce-scatter.2.cloned.1.call-update
  669.7 0.0 copy-done.2
  669.7 0.1 broadcast_add_fusion
  669.8 0.1 add.95
  669.9 0.0 copy-done.3
  669.9 0.0 slice-done
  669.9 0.1 add_bitcast_fusion
  670.0 0.1 dynamic_slice.3
  670.0 205.1 %reduce-scatter.2.cloned.1.call-done = f32[64,1024]{1,0:T(8,128)} async-done(((f32[1024,1024]{1,0:T(8,128)}), f32[64,1024]{1,0:T(8,128)}) %reduce-scatter.2.cloned.1.call-update) | async-done | bytes 262160 | tf_op jit(solution)/shard_map/reduce_scatter | solution.py:40
  875.2 1.8 subtract_divide_fusion
  (9 shorter events, 0.0 us)
Async XLA Ops:
  29.4 7.6 copy-start
  29.4 7.8 copy-start.1
  29.4 596.4 %all-to-all-start = ((bf16[64,16,16384]{2,0,1:T(8,128)(2,1)}), bf16[64,16,16384]{2,0,1:T(8,128)(2,1)}, u32[]{:S(2)}, u32[]{:S(2)}) async-start(bf16[64,16,16384]{2,0,1:T(8,128)(2,1)} %bitcast.13), calls=%async_computation | async-start | bytes 67108864 | tf_op jit(solution)/shard_map/all_to_all | solution.py:28
  36.9 838.2 %reduce-scatter.2.cloned.1.call-start = ((), (), s32[]{:S(2)}) async-start(), calls=%async_computation.2 | async-start | bytes 4456448 | tf_op jit(solution)/shard_map/reduce_scatter | solution.py:40
  625.8 43.9 %copy-start.2 = (f32[32]{0:T(128)S(1)}, f32[32]{0:T(128)}, u32[]{:S(2)}) copy-start(f32[32]{0:T(128)} %param.10) | copy-start | bytes 388
  625.8 44.1 %copy-start.3 = (f32[512]{0:T(512)S(1)}, f32[512]{0:T(512)}, u32[]{:S(2)}) copy-start(f32[512]{0:T(512)} %param.11) | copy-start | bytes 6148
  625.8 44.1 %slice-start = ((f32[512]{0:T(512)}), f32[2]{0:T(128)S(1)}, s32[]{:S(2)}) async-start(f32[512]{0:T(512)} %param.11), calls=%async_computation.3 | async-start | bytes 1024 | tf_op jit(solution)/shard_map/slice | solution.py:41
Sparse Core Ops, SparseCore 0:
  669.9 205.2 reduce-scatter.1
where the time goes:
time: 884 us
  waiting for transfers between devices  793 us (90%)
  matrix products  43.9 us (5%)
  local copies, waits for them, and re-layouts  23.1 us (3%)
  between operations  13.5 us (2%)
    all_to_all x1, waiting for transfers between devices, body(): lax.all_to_all(amplitudes, 'wide', split_axis=1, concat_axis=0, tiled=True)  588 us
    reduce_scatter x1, waiting for transfers between devices, body(): lax.psum_scatter(contract(kept_t, kept_v), 'wide', scatter_dimension=0, t...  205 us
    dot_general x1, matrix products, contract(): lax.dot_general(left, right, (((1,), (1,)), ((), ())), preferred_element_...  43.9 us
    all_to_all x1, local copies, waits for them, and re-layouts, body(): lax.all_to_all(amplitudes, 'wide', split_axis=1, concat_axis=0, tiled=True)  22.8 us
  transfers between devices with their start and end apart: 2, of which 2 were waited for; matrix products, arithmetic and copies ran while one was open for 0% of the time, Pallas kernels for 0%

commit v1 on v0

--- a/solution.py
+++ b/solution.py
@@ -1,9 +1,28 @@
 import jax
 import jax.numpy as jnp
 from jax import lax
+from jax.experimental import pallas as pl
+from jax.experimental.pallas import tpu as pltpu
 from jax.sharding import PartitionSpec as P
 
 BLK = 64
+LANE = 128
+SUB = 8
+NBLK = 8
+CORES = 2
+ROWCAP = 256
+CHUNKS = ((0, 4), (16, 16), (8, 8), (4, 4))
+LEVELS = ((96, 24), (128, 24))
+MOST = max(cap for cap, _ in LEVELS)
+CHIP, CORE, PURE, TILE_A, TILE_B, ROLL, TILE_U, TILE_W, HALF, KIND, ROLE, LEVEL = 0, 1, 2, 4, 5, 6, 7, 8, 9, 16, 24, 27
+START, COUNT, ROW_CLASS, ROW_RANK, SIZE = 32, 96, 128, 192, 256
+TYPES = ((0, 1, 2), (1, 0, 3), (2, 3, 0))
+SMEM = pltpu.SMEM
+VMEM = pltpu.VMEM
+GRANT = 48 * 1024 * 1024
+BF = jnp.bfloat16
+F32 = jnp.float32
+I32 = jnp.int32
 
 
 def block_lookup(table, block_ids):
@@ -18,7 +37,7 @@
     )
 
 
-def body(amplitudes, integrals, occ_irrep, vir_irrep, occ_energy, vir_energy):
+def dense_body(amplitudes, integrals, occ_irrep, vir_irrep, occ_energy, vir_energy):
     position = lax.axis_index("wide")
     pairs_local = amplitudes.shape[0]
     local_cols = integrals.shape[1]
@@ -47,6 +66,489 @@
     return summed / denominator
 
 
+def tile(ref, lead, c, which):
+    start = pl.multiple_of(c * NBLK * BLK + which * LANE, LANE)
+    return ref[lead + (slice(None), pl.ds(start, LANE))]
+
+
+def maybe_roll(x, flag):
+    return jnp.where(flag == 1, jnp.concatenate([x[:, BLK:], x[:, :BLK]], axis=1), x)
+
+
+def half_masks(table, shape):
+    half = (lax.broadcasted_iota(I32, shape, 1) % LANE) // BLK
+    first = half == table[HALF]
+    return jnp.where(first, 1.0, 0.0).astype(BF), jnp.where(first, 0.0, 1.0).astype(BF)
+
+
+def setup_kernel(
+    devices, nslab, place, occ, vir, occ_here, occ_lane, occ_rows, table, pick_ref, big_ref, a_ref, b_ref, class_ref, hist, tally
+):
+    chips = devices // CORES
+    nocc = occ.shape[0]
+    per_device = nocc // devices
+    chip, core = place[0], place[1]
+    table[CHIP] = chip
+    table[CORE] = core
+    common, zero_at, seven_at = vir[0] * 0, vir[0] * 0, vir[0] * 0
+    for b in range(NBLK):
+        label = vir[b]
+        common = jnp.where((label != 0) & (label != 7), label, common)
+        zero_at = jnp.where(label == 0, b, zero_at)
+        seven_at = jnp.where(label == 7, b, seven_at)
+        table[KIND + b] = jnp.where(label == 0, 1, jnp.where(label == 7, 2, 0))
+    irreps = [common * 0, common, common ^ 7, common * 0 + 7]
+    needed = []
+    for g in range(4):
+        some = common * 0
+        for b in range(NBLK):
+            some = jnp.where((vir[0] ^ vir[b]) == irreps[g], 1, some)
+        needed.append(some)
+
+    tile_a, half_a = zero_at // 2, zero_at % 2
+    same = seven_at // 2 == tile_a
+    tile_b = jnp.where(same, (tile_a + 1) % 4, seven_at // 2)
+    pure = jnp.where((tile_a != 0) & (tile_b != 0), 0, jnp.where((tile_a != 1) & (tile_b != 1), 1, 2))
+    table[PURE] = pure
+    table[PURE + 1] = 6 - tile_a - tile_b - pure
+    table[TILE_A] = tile_a
+    table[TILE_B] = tile_b
+    table[ROLL] = jnp.where(same | (seven_at % 2 != half_a), 0, 1)
+    table[TILE_U] = jnp.where(same, tile_a, tile_b)
+    table[TILE_W] = jnp.where(same, tile_b, tile_a)
+    table[HALF] = half_a
+
+    for h in range(NBLK):
+        hist[h] = 0
+    for j in range(nocc):
+        hist[NBLK + j] = hist[occ[j]]
+        hist[occ[j]] = hist[occ[j]] + 1
+    of_i = lambda i, g: hist[occ[i] ^ irreps[g]] * needed[g]
+    biggest = common * 0
+    most_class = common * 0
+    for g in range(4):
+        total = common * 0
+        for s in range(devices):
+            table[START + g * devices + s] = total
+            here = common * 0
+            for i in range(per_device):
+                here += of_i(s * per_device + i, g)
+            total += here
+            biggest = jnp.maximum(biggest, here)
+            tally[g * devices + s] = here
+        most_class = jnp.maximum(most_class, total)
+        for c in range(chips):
+            table[COUNT + g * chips + c] = tally[g * devices + c * CORES] + tally[g * devices + c * CORES + 1]
+    most = common * 0
+    for c in range(chips):
+        n = [table[COUNT + g * chips + c] for g in range(4)]
+        for b, a, s in TYPES:
+            most = jnp.maximum(most, 3 * n[b] + jnp.maximum(n[a], n[s]))
+    level = common * 0 + len(LEVELS)
+    for at in range(len(LEVELS) - 1, -1, -1):
+        cap, cap_back = LEVELS[at]
+        level = jnp.where((most <= cap) & (biggest <= cap_back) & (most_class <= ROWCAP), at, level)
+    table[LEVEL] = level
+
+    my_kind = table[KIND + chip]
+    roles = [jnp.where(my_kind == 0, x, jnp.where(my_kind == 1, y, z)) for x, y, z in zip(*TYPES)]
+    for n in range(3):
+        table[ROLE + n] = roles[n]
+    position = chip * CORES + core
+    for i in range(per_device):
+        at = position * per_device + i
+        for j in range(nocc):
+            both = occ[at] ^ occ[j]
+            kind = common * 0 + 4
+            rank = hist[NBLK + j]
+            for g in range(4):
+                hit = (both == irreps[g]) & (needed[g] == 1)
+                kind = jnp.where(hit, g, kind)
+                for before in range(i):
+                    rank = rank + jnp.where(hit, of_i(position * per_device + before, g), 0)
+            table[ROW_CLASS + i * nocc + j] = kind
+            table[ROW_RANK + i * nocc + j] = rank
+
+    width = CORES * per_device * nocc
+    lane = lax.broadcasted_iota(I32, (1, width), 1)
+    earlier = lax.broadcasted_iota(I32, (nocc, width), 0) < lax.broadcasted_iota(I32, (nocc, width), 1) % nocc
+    alike = jnp.where((occ_rows[...] == occ_lane[...]) & earlier, 1, 0)
+    rank = jnp.sum(alike, axis=0, keepdims=True)
+    irrep = occ_lane[...] ^ occ_here[...]
+    spots = []
+    for g in range(4):
+        base, run = jnp.zeros((1, width), I32), common * 0
+        for i in range(CORES * per_device):
+            shown = i ^ (core * per_device)
+            base = jnp.where(lane // nocc == shown, run, base)
+            run += of_i(chip * CORES * per_device + i, g)
+        spots.append((jnp.where((irrep == irreps[g]) & (needed[g] == 1), base + rank, -4 * MOST), run))
+    slot = lax.broadcasted_iota(I32, (MOST, width), 0)
+    for t, (b, a, s) in enumerate(TYPES):
+        for section, (g, f) in enumerate(((b, 0), (b, 1), (b, 2), (a, 3), (s, 3))):
+            target = spots[g][0] + f * spots[b][1]
+            pick_ref[t, :, section * width : (section + 1) * width] = jnp.where(slot == target, 1.0, 0.0).astype(BF)
+
+    half = lax.broadcasted_iota(I32, (BLK, LANE), 1) // BLK == half_a
+    column = lax.broadcasted_iota(I32, class_ref.shape, 1) % (NBLK * BLK) // BLK
+    column_class = jnp.zeros(class_ref.shape, I32)
+    for b in range(NBLK):
+        both = vir[0] ^ vir[b]
+        kind = common * 0 + 4
+        for g in range(4):
+            kind = jnp.where(both == irreps[g], g, kind)
+        column_class = jnp.where(column == b, kind, column_class)
+        is_ = [jnp.where(kind == roles[n], 1.0, 0.0) for n in range(3)]
+        full = jnp.zeros((BLK, LANE), F32)
+        for a in range(nslab):
+            rows = slice((a * NBLK + b) * BLK, (a * NBLK + b + 1) * BLK)
+            big_ref[rows, :] = (full + is_[0]).astype(BF)
+            a_ref[rows, :] = jnp.where(half, full + is_[1], 0.0).astype(BF)
+            b_ref[rows, :] = jnp.where(half, 0.0, full + is_[2]).astype(BF)
+    class_ref[...] = column_class
+
+
+def setup(place, occ, vir, slab_rows, devices):
+    nocc = occ.shape[0]
+    width = CORES * nocc // devices * nocc
+    per_chip = width // nocc
+    chip, core = place[0], place[1]
+    mine = lax.dynamic_slice_in_dim(occ, chip * per_chip, per_chip, 0).reshape(CORES, -1)
+    mine = jnp.where(core == 0, mine, mine[::-1]).reshape(-1)
+    occ_here = jnp.repeat(mine, nocc)[None, :]
+    occ_lane = jnp.tile(occ, per_chip)[None, :]
+    occ_rows = jnp.broadcast_to(occ[:, None], (nocc, width))
+    smem, vmem = pl.BlockSpec(memory_space=SMEM), pl.BlockSpec(memory_space=VMEM)
+    mask = jax.ShapeDtypeStruct((slab_rows, LANE), BF)
+    return pl.pallas_call(
+        lambda *refs: setup_kernel(devices, slab_rows // (NBLK * BLK), *refs),
+        in_specs=[smem] * 3 + [vmem] * 3,
+        out_specs=[smem] + [vmem] * 5,
+        out_shape=[
+            jax.ShapeDtypeStruct((SIZE,), I32),
+            jax.ShapeDtypeStruct((3, MOST, 5 * width), BF),
+            mask,
+            mask,
+            mask,
+            jax.ShapeDtypeStruct((1, slab_rows), I32),
+        ],
+        scratch_shapes=[SMEM((NBLK + nocc,), I32), SMEM((4 * devices,), I32)],
+        name="setup",
+    )(place, occ, vir, occ_here, occ_lane, occ_rows)
+
+
+def take_kernel(chips, table, *refs):
+    for d in range(chips):
+        refs[chips][d] = refs[d][...]
+
+
+def take_for_sibling(table, amplitudes, first, count, cols_device):
+    rows, width = amplitudes.shape[0], count * NBLK * BLK
+    chips = amplitudes.shape[1] // cols_device // CORES
+    step = 2 * NBLK * BLK
+    per_device = cols_device // step
+
+    def column(d):
+        return lambda q, s: (0, ((s[CHIP] ^ d) * CORES + 1 - s[CORE]) * per_device + first // 2 + q)
+
+    return pl.pallas_call(
+        lambda *refs: take_kernel(chips, *refs),
+        grid_spec=pltpu.PrefetchScalarGridSpec(
+            num_scalar_prefetch=1,
+            grid=(width // step,),
+            in_specs=[pl.BlockSpec((rows, step), column(d)) for d in range(chips)],
+            out_specs=pl.BlockSpec((chips, rows, step), lambda q, s: (0, 0, q)),
+        ),
+        out_shape=jax.ShapeDtypeStruct((chips, rows, width), amplitudes.dtype),
+        cost_estimate=pl.CostEstimate(flops=0, bytes_accessed=4 * chips * rows * width, transcendentals=0),
+        name="take_for_sibling",
+    )(table, *[amplitudes] * chips)
+
+
+def pack_kernel(count, chips, table, own_ref, sib_ref, pick_ref, *rest):
+    outs, held = rest[:chips], rest[chips]
+    d = pl.program_id(0)
+    pick = pick_ref[0]
+    mine, other = half_masks(table, (own_ref.shape[0], LANE))
+    for u in range(count // 2):
+        columns = []
+        for c in (2 * u, 2 * u + 1):
+            parts = [[], [], [], [], []]
+            for ref, lead in ((own_ref, ()), (sib_ref, (0,))):
+                at = lambda n: tile(ref, lead, c, table[n])
+                parts[0].append(at(PURE))
+                parts[1].append(at(PURE + 1))
+                parts[2].append(at(TILE_W) * other + maybe_roll(at(TILE_B), table[ROLL]) * mine)
+                parts[3].append(at(TILE_A) * mine)
+                parts[4].append(maybe_roll(at(TILE_U), table[ROLL]) * other)
+            columns.append(jnp.concatenate([x for part in parts for x in part], axis=0))
+        rows = jnp.concatenate(columns, axis=1)
+        held[:, u * 2 * LANE : (u + 1) * 2 * LANE] = jnp.dot(pick, rows, preferred_element_type=F32).astype(BF)
+    for i in range(chips):
+
+        @pl.when(d == i)
+        def _():
+            outs[i][...] = held[...]
+
+
+def pack(table, amplitudes, sibling, pick, cap, first, count, cols_device):
+    rows, width = amplitudes.shape[0], count * NBLK * BLK
+    chips = amplitudes.shape[1] // cols_device // CORES
+    per_device = cols_device // width
+
+    def column(d, s):
+        return (0, ((s[CHIP] ^ d) * CORES + s[CORE]) * per_device + first // count)
+
+    out = jax.ShapeDtypeStruct((cap, count * LANE), BF)
+    return pl.pallas_call(
+        lambda *refs: pack_kernel(count, chips, *refs),
+        grid_spec=pltpu.PrefetchScalarGridSpec(
+            num_scalar_prefetch=1,
+            grid=(chips,),
+            in_specs=[
+                pl.BlockSpec((rows, width), column),
+                pl.BlockSpec((1, rows, width), lambda d, s: (d, 0, 0)),
+                pl.BlockSpec((1, cap, pick.shape[2]), lambda d, s: (s[KIND + (s[CHIP] ^ d)], 0, 0)),
+            ],
+            out_specs=[pl.BlockSpec(out.shape, lambda d, s: (0, 0))] * chips,
+            scratch_shapes=[pltpu.VMEM(out.shape, BF)],
+        ),
+        out_shape=[out] * chips,
+        compiler_params=pltpu.CompilerParams(vmem_limit_bytes=GRANT),
+        cost_estimate=pl.CostEstimate(
+            flops=2 * chips * count * LANE * cap * 10 * rows,
+            bytes_accessed=4 * chips * rows * width + 2 * chips * cap * count * LANE,
+            transcendentals=0,
+        ),
+        name="pack",
+    )(table, amplitudes, sibling, pick)
+
+
+def spread_kernel(chips, cap, table, spread_ref):
+    column = lax.broadcasted_iota(I32, (1, chips * cap), 1)
+    row = lax.broadcasted_iota(I32, (ROWCAP, chips * cap), 0)
+    for section, (n, f) in enumerate(((0, 0), (0, 1), (0, 2), (1, 3), (2, 3))):
+        target = jnp.full((1, chips * cap), -1, I32)
+        for d in range(chips):
+            chip = table[CHIP] ^ d
+            group = table[ROLE + n]
+            k = column - d * cap - f * table[COUNT + table[ROLE] * chips + chip]
+            count = table[COUNT + group * chips + chip]
+            start = table[START + (group * chips + chip) * CORES]
+            inside = (column >= d * cap) & (column < (d + 1) * cap) & (k >= 0) & (k < count)
+            target = jnp.where(inside, start + k, target)
+        spread_ref[section * ROWCAP : (section + 1) * ROWCAP, :] = jnp.where(row == target, 1.0, 0.0).astype(BF)
+
+
+def make_spread(table, chips, cap):
+    return pl.pallas_call(
+        lambda *refs: spread_kernel(chips, cap, *refs),
+        in_specs=[pl.BlockSpec(memory_space=SMEM)],
+        out_specs=pl.BlockSpec(memory_space=VMEM),
+        out_shape=jax.ShapeDtypeStruct((5 * ROWCAP, chips * cap), BF),
+        compiler_params=pltpu.CompilerParams(vmem_limit_bytes=GRANT),
+        cost_estimate=pl.CostEstimate(flops=0, bytes_accessed=10 * ROWCAP * chips * cap, transcendentals=0),
+        name="make_spread",
+    )(table)
+
+
+def contract_kernel(chips, table, *refs):
+    parts, (vals, spread_ref, big_ref, a_ref, b_ref, acc_ref, out_ref) = refs[:chips], refs[chips:]
+
+    @pl.when(pl.program_id(0) == 0)
+    def _():
+        out_ref[...] = acc_ref[...]
+
+    received = jnp.concatenate([r[...] for r in parts], axis=0)
+    spread = jnp.dot(spread_ref[...], received, preferred_element_type=F32)
+    left = [spread[j * ROWCAP : (j + 1) * ROWCAP] for j in range(5)]
+    half = (lax.broadcasted_iota(I32, (ROWCAP, 2 * LANE), 1) % LANE) // BLK
+    left = [x.astype(BF) for x in left[:3] + [jnp.where(half == table[HALF], left[3], left[4])]]
+    mine, other = half_masks(table, (vals.shape[0], LANE))
+    right = [[], [], [], []]
+    for c in (0, 1):
+        at = lambda n: tile(vals, (), c, table[n])
+        right[0].append(at(PURE) * big_ref[...])
+        right[1].append(at(PURE + 1) * big_ref[...])
+        right[2].append((at(TILE_W) * other + maybe_roll(at(TILE_B), table[ROLL]) * mine) * big_ref[...])
+        right[3].append(at(TILE_A) * a_ref[...] + maybe_roll(at(TILE_U), table[ROLL]) * b_ref[...])
+    total = out_ref[...]
+    for j in range(4):
+        total += contract(jnp.concatenate(right[j], axis=1), left[j])
+    out_ref[...] = total
+
+
+def contract_chunk(table, received, integrals, spread, masks, acc, first, count):
+    chips = len(received)
+    cap = received[0].shape[0]
+    slab = integrals.shape[0]
+    fixed = lambda u, s: (0, 0)
+    return pl.pallas_call(
+        lambda *refs: contract_kernel(chips, *refs),
+        grid_spec=pltpu.PrefetchScalarGridSpec(
+            num_scalar_prefetch=1,
+            grid=(count // 2,),
+            in_specs=[pl.BlockSpec((cap, 2 * LANE), lambda u, s: (0, u))] * chips
+            + [pl.BlockSpec((slab, 2 * NBLK * BLK), lambda u, s: (0, first // 2 + u))]
+            + [pl.BlockSpec(x.shape, fixed) for x in (spread, *masks, acc)],
+            out_specs=pl.BlockSpec(acc.shape, fixed),
+        ),
+        out_shape=jax.ShapeDtypeStruct(acc.shape, F32),
+        compiler_params=pltpu.CompilerParams(vmem_limit_bytes=GRANT),
+        cost_estimate=pl.CostEstimate(
+            flops=2 * count * LANE * (5 * ROWCAP * chips * cap + 4 * ROWCAP * slab),
+            bytes_accessed=2 * slab * count * NBLK * BLK + 8 * acc.shape[0] * slab,
+            transcendentals=0,
+        ),
+        name="contract_chunk",
+    )(table, *received, integrals, spread, *masks, acc)
+
+
+def split_kernel(chips, cap, table, sums_ref, class_ref, own_ref, sib_ref, held):
+    d = pl.program_id(0)
+
+    @pl.when(d == 0)
+    def _():
+        held[:ROWCAP, :] = sums_ref[...].T
+        held[ROWCAP:, :] = jnp.zeros((cap + SUB, held.shape[1]), F32)
+
+    for flip, ref in ((0, own_ref), (1, sib_ref)):
+        device = (table[CHIP] ^ d) * CORES + (table[CORE] ^ flip)
+        rows = []
+        for g in range(4):
+            start = table[START + g * chips * CORES + device]
+            odd = start % SUB
+            window = held[pl.ds(pl.multiple_of(start - odd, SUB), cap + SUB), :]
+            rows.append(pltpu.roll(window, (cap + SUB - odd) % (cap + SUB), 0)[:cap])
+        kind = class_ref[...]
+        ref[0] = jnp.where(kind == 0, rows[0], jnp.where(kind == 1, rows[1], jnp.where(kind == 2, rows[2], rows[3])))
+
+
+def split(table, sums, column_class, chips, cap):
+    slab = sums.shape[0]
+    out = jax.ShapeDtypeStruct((chips, cap, slab), F32)
+    fixed = lambda d, s: (0, 0)
+    return pl.pallas_call(
+        lambda *refs: split_kernel(chips, cap, *refs),
+        grid_spec=pltpu.PrefetchScalarGridSpec(
+            num_scalar_prefetch=1,
+            grid=(chips,),
+            in_specs=[pl.BlockSpec(sums.shape, fixed), pl.BlockSpec((1, slab), fixed)],
+            out_specs=[pl.BlockSpec((1, cap, slab), lambda d, s: (d, 0, 0))] * 2,
+            scratch_shapes=[pltpu.VMEM((ROWCAP + cap + SUB, slab), F32)],
+        ),
+        out_shape=[out, out],
+        cost_estimate=pl.CostEstimate(flops=0, bytes_accessed=4 * sums.size + 8 * out.size, transcendentals=0),
+        name="split_sums",
+    )(table, sums, column_class)
+
+
+def add_kernel(own_ref, sib_ref, *outs):
+    for d, ref in enumerate(outs):
+        ref[...] = own_ref[d] + sib_ref[d]
+
+
+def add_cores(own, sibling):
+    out = jax.ShapeDtypeStruct(own.shape[1:], F32)
+    return pl.pallas_call(
+        add_kernel,
+        out_shape=[out] * own.shape[0],
+        cost_estimate=pl.CostEstimate(flops=own.size, bytes_accessed=12 * own.size, transcendentals=0),
+        name="add_cores",
+    )(own, sibling)
+
+
+def finish_kernel(count, pairs, table, energies, class_ref, slab_ref, *refs):
+    parts, out_ref, held = refs[:count], refs[count], refs[count + 1]
+    total = parts[0][...]
+    for ref in parts[1:]:
+        total = total + ref[...]
+    held[...] = total
+    for p in range(pairs):
+        kind = table[ROW_CLASS + p]
+        row = held[pl.ds(jnp.where(kind < 4, table[ROW_RANK + p], 0), 1), :]
+        kept = jnp.where(class_ref[...] == kind, row, 0.0)
+        out_ref[p : p + 1, :] = kept / (slab_ref[...] - energies[p])
+
+
+def finish(table, parts, energies, column_class, slab_energy):
+    pairs, slab = energies.shape[0], column_class.shape[1]
+    smem, vmem = pl.BlockSpec(memory_space=SMEM), pl.BlockSpec(memory_space=VMEM)
+    return pl.pallas_call(
+        lambda *refs: finish_kernel(len(parts), pairs, *refs),
+        in_specs=[smem] * 2 + [vmem] * (2 + len(parts)),
+        out_specs=vmem,
+        out_shape=jax.ShapeDtypeStruct((pairs, slab), F32),
+        scratch_shapes=[pltpu.VMEM(parts[0].shape, F32)],
+        cost_estimate=pl.CostEstimate(flops=4 * pairs * slab, bytes_accessed=8 * pairs * slab, transcendentals=0),
+        name="finish",
+    )(table, energies, column_class, slab_energy, *parts)
+
+
+def body(amplitudes, integrals, occ_irrep, vir_irrep, occ_energy, vir_energy):
+    devices = lax.axis_size("wide")
+    pairs_local = amplitudes.shape[0]
+    cols = integrals.shape[1]
+    slab_rows = integrals.shape[0]
+    nvir = vir_energy.shape[0]
+    nocc = occ_irrep.shape[0]
+    given = (amplitudes, integrals, occ_irrep, vir_irrep, occ_energy, vir_energy)
+    compact = (
+        nvir == NBLK * BLK
+        and CORES * cols == BLK * nvir
+        and cols == sum(count for _, count in CHUNKS) * nvir
+        and pairs_local % 16 == 0
+        and devices == 16
+        and nocc == 32
+        and devices * pairs_local == nocc * nocc
+        and lax.axis_size("parts") == 2
+    )
+    if not compact:
+        return dense_body(*given)
+
+    chips = devices // CORES
+    position = lax.axis_index("wide")
+    place = jnp.stack([position // CORES, position % CORES]).astype(I32)
+    swap = [(i, i ^ 1) for i in range(devices)]
+    routes = [[(i, i ^ (d * CORES)) for i in range(devices)] for d in range(chips)]
+    table, pick, big, mask_a, mask_b, column_class = setup(place, occ_irrep, vir_irrep, slab_rows, devices)
+    level = table[LEVEL : LEVEL + 1]
+    level = jnp.maximum(level, lax.ppermute(level, "parts", [(0, 1), (1, 0)]))[0]
+
+    def from_sibling(first, count):
+        return lax.ppermute(take_for_sibling(place, amplitudes, first, count, cols), "wide", swap)
+
+    early = from_sibling(*CHUNKS[0])
+
+    def compact_plan(cap, cap_back):
+        def run(amplitudes, integrals, early):
+            spread = make_spread(table, chips, cap)
+            sent = []
+            for n, (first, count) in enumerate(CHUNKS):
+                sibling = early if n == 0 else from_sibling(first, count)
+                packed = pack(table, amplitudes, sibling, pick, cap, first, count, cols)
+                received = [packed[0]] + [lax.ppermute(packed[d], "wide", routes[d]) for d in range(1, chips)]
+                sent.append((received, first, count))
+            acc = jnp.zeros((slab_rows, ROWCAP), F32)
+            for received, first, count in sent:
+                acc = contract_chunk(table, received, integrals, spread, (big, mask_a, mask_b), acc, first, count)
+            own, other = split(table, acc, column_class, chips, cap_back)
+            halves = add_cores(own, lax.ppermute(other, "wide", swap))
+            back = [halves[0]] + [lax.ppermute(halves[d], "wide", routes[d]) for d in range(1, chips)]
+            slab_energy = (vir_energy[: slab_rows // nvir, None] + vir_energy[None, :]).reshape(1, -1)
+            pair_energy = (occ_energy[:, None] + occ_energy[None, :]).reshape(-1)
+            own_energy = lax.dynamic_slice_in_dim(pair_energy, position * pairs_local, pairs_local, 0)
+            return finish(table, back, own_energy, column_class, slab_energy)
+
+        return run
+
+    def dense_plan(amplitudes, integrals, early):
+        return dense_body(amplitudes, integrals, *given[2:])
+
+    plans = [compact_plan(n, m) for n, m in LEVELS] + [dense_plan]
+    return lax.switch(level, plans, amplitudes, integrals, early)
+
+
 def solution(mesh):
     return jax.shard_map(
         body,

time: 884 us -> 345 us (0.39)
  waiting for transfers between devices: 793 us -> 83.3 us
  Pallas kernels: 0 us -> 124 us
  starting transfers between devices: 7.59 us -> 95.7 us
  matrix products: 43.9 us -> 0 us
  local copies, waits for them, and re-layouts: 23.1 us -> 9.97 us
  loops' own time: 0 us -> 10.2 us
    all_to_all x1 -> x0, waiting for transfers between devices: 588 us -> none  [body(): lax.all_to_all(amplitudes, 'wide', split_axis=1, concat_axis=0, tiled=True)]
    reduce_scatter x1 -> x0, waiting for transfers between devices: 205 us -> none  [body(): lax.psum_scatter(contract(kept_t, kept_v), 'wide', scatter_dimension=0, t...]
    pallas_call x0 -> x17, Pallas kernels: none -> 124 us  [the longest x4 51 us: contract_chunk(): pl.pallas_call(lambda *refs: contract_kernel(chips, *refs), grid_spec=plt...]
    ppermute x0 -> x41, starting transfers between devices: none -> 95.7 us  [the longest x28 80.9 us: run(): lax.ppermute(packed[d], 'wide', routes[d])]
    ppermute x0 -> x41, waiting for transfers between devices: none -> 83.3 us  [the longest x28 71.9 us: run(): lax.ppermute(packed[d], 'wide', routes[d])]
    dot_general x1 -> x0, matrix products: 43.9 us -> none  [contract(): lax.dot_general(left, right, (((1,), (1,)), ((), ())), preferred_element_...]
    all_to_all x1 -> x0, local copies, waits for them, and re-layouts: 22.8 us -> none  [body(): lax.all_to_all(amplitudes, 'wide', split_axis=1, concat_axis=0, tiled=True)]
    another operation x0 -> x1, loops' own time: none -> 10.2 us  [body(): return lax.switch(level, plans, amplitudes, integrals, early)]
  transfers between devices with their start and end apart: 2 -> 41, of which waited for: 2 -> 8; matrix products, arithmetic and copies ran while one was open for 0% -> 1% of each run, Pallas kernels for 0% -> 28%
where the time goes in v1:
time: 345 us; the launch traced here: 338 us
  Pallas kernels  124 us (36%)
  starting transfers between devices  95.7 us (28%)
  waiting for transfers between devices  83.3 us (24%)
  between operations  15.2 us (4%)
  loops' own time  10.2 us (3%)
  local copies, waits for them, and re-layouts  9.97 us (3%)
    ppermute x28, starting transfers between devices, run(): lax.ppermute(packed[d], 'wide', routes[d])  80.9 us
    ppermute x28, waiting for transfers between devices, run(): lax.ppermute(packed[d], 'wide', routes[d])  71.9 us
    pallas_call x4, Pallas kernels, contract_chunk(): pl.pallas_call(lambda *refs: contract_kernel(chips, *refs), grid_spec=plt...  51 us
    pallas_call x4, Pallas kernels, pack(): pl.pallas_call(lambda *refs: pack_kernel(count, chips, *refs), grid_spec=...  37.4 us
    pallas_call x4, Pallas kernels, take_for_sibling(): pl.pallas_call(lambda *refs: take_kernel(chips, *refs), grid_spec=pltpu.P...  21.7 us
    ppermute x7, starting transfers between devices, run(): lax.ppermute(halves[d], 'wide', routes[d])  11.2 us
    another operation x1, loops' own time, body(): return lax.switch(level, plans, amplitudes, integrals, early)  10.2 us
    ppermute x7, waiting for transfers between devices, run(): lax.ppermute(halves[d], 'wide', routes[d])  7.21 us
  transfers between devices with their start and end apart: 41, of which 8 were waited for; matrix products, arithmetic and copies ran while one was open for 1% of the time, Pallas kernels for 28%

profile of v1, /device:TPU:0, one launch (start us, length us, event | category | flops | bytes accessed | tf_op | source)
XLA Modules:
  0.0 338.1 jit_solution(12382307548637321753)
XLA Ops:
  6.6 3.4 take_for_sibling.13
  23.1 307.0 %conditional.1 = (f32[64,1024]{1,0:T(8,128)S(1)}) conditional(s32[]{:T(128)} %bitcast.4, (f32[32]{0:T(128)S(1)}, s32[]{:T(128)}, f32[512]{0:T(512)}, s32[2]{0:T(128)S(1)}, bf16[64,262144]{1,0:T(8,128)(2,1)}, /*index=5*/s32[256]{0:T(256)}, bf16[3,128,640]{2,1,0:T(8,128)(2,1)}, bf16[8,64,2048]{2,1,0:T(8,128)(2,1)}, ...), branch_computations={%region_0.1_spmd, %region_1.2_spmd, %region_2.7_spmd} | conditional | flops 34428583936 | bytes 290383552 | solution.py:549
  31.5 9.6 %take_for_sibling.12 = bf16[8,64,8192]{2,1,0:T(8,128)(2,1)} custom-call(s32[2]{0:T(128)S(1)} %get-tuple-element.134.refs_0_, bf16[64,262144]{1,0:T(8,128)(2,1)} %get-tuple-element.133.refs_1_.refs_2_.refs_3_.refs_4_.refs_5_.refs_6_.refs_7_.refs_8_, bf16[64,262144]{1,0:T(8,128)(2,1)} %get-tuple-element.133.refs_1_.refs_2_.refs_3_.refs_4_.refs_5_.refs_6_.refs_7_.refs_8_, ...), custom_call_target="tpu_custom_call" | custom-call | bytes 16777216 | tf_op jit(solution)/shard_map/cond/branch_1_fun/take_for_sibling/pallas_call | solution.py:254
  41.2 5.5 %take_for_sibling.11 = bf16[8,64,4096]{2,1,0:T(8,128)(2,1)} custom-call(s32[2]{0:T(128)S(1)} %get-tuple-element.134.refs_0_, bf16[64,262144]{1,0:T(8,128)(2,1)} %get-tuple-element.133.refs_1_.refs_2_.refs_3_.refs_4_.refs_5_.refs_6_.refs_7_.refs_8_, bf16[64,262144]{1,0:T(8,128)(2,1)} %get-tuple-element.133.refs_1_.refs_2_.refs_3_.refs_4_.refs_5_.refs_6_.refs_7_.refs_8_, ...), custom_call_target="tpu_custom_call" | custom-call | bytes 8388608 | tf_op jit(solution)/shard_map/cond/branch_1_fun/take_for_sibling/pallas_call | solution.py:254
  47.2 3.3 take_for_sibling.10
  50.6 6.9 %pack.15 = (bf16[128,512]{1,0:T(8,128)(2,1)S(1)}, bf16[128,512]{1,0:T(8,128)(2,1)S(1)}, bf16[128,512]{1,0:T(8,128)(2,1)S(1)}, bf16[128,512]{1,0:T(8,128)(2,1)S(1...) custom-call(s32[256]{0:T(256)S(1)} %copy-done.22, ...), custom_call_target="tpu_custom_call" | custom-call | flops 671088640 | bytes 5242880 | tf_op jit(solution)/shard_map/cond/branch_1_fun/pack/pallas_call | solution.py:303
  69.3 13.9 %pack.14 = (bf16[128,2048]{1,0:T(8,128)(2,1)S(1)}, bf16[128,2048]{1,0:T(8,128)(2,1)S(1)}, bf16[128,2048]{1,0:T(8,128)(2,1)S(1)}, bf16[128,2048]{1,0:T(8,128)(2,1...) custom-call(s32[256]{0:T(256)S(1)} %copy-done.22, ...), custom_call_target="tpu_custom_call" | custom-call | flops 2684354560 | bytes 20971520 | tf_op jit(solution)/shard_map/cond/branch_1_fun/pack/pallas_call | solution.py:303
  85.2 3.6 %collective-permute-start.68 = (bf16[128,512]{1,0:T(8,128)(2,1)S(1)}, bf16[128,512]{1,0:T(8,128)(2,1)S(1)}, u32[]{:S(2)}, u32[]{:S(2)}) collective-permute-start(bf16[128,512]{1,0:T(8,128)(2,1)S(1)} %get-tuple-element.171), channel_id=1, source_target_pairs={{0,12},{1,13},{2,14},{3,15},{4,8},{5,9},{6,10},{7,11},{8,4},{9,5},... | collective-permute-start | bytes 393224 | tf_op jit(solution)/shard_map/cond/branch_1_fun/ppermute | solution.py:530
  88.9 6.9 %pack.12 = (bf16[128,512]{1,0:T(8,128)(2,1)S(1)}, bf16[128,512]{1,0:T(8,128)(2,1)S(1)}, bf16[128,512]{1,0:T(8,128)(2,1)S(1)}, bf16[128,512]{1,0:T(8,128)(2,1)S(1...) custom-call(s32[256]{0:T(256)S(1)} %copy-done.22, ...), custom_call_target="tpu_custom_call" | custom-call | flops 671088640 | bytes 5242880 | tf_op jit(solution)/shard_map/cond/branch_1_fun/pack/pallas_call | solution.py:303
  97.5 9.8 %pack.13 = (bf16[128,1024]{1,0:T(8,128)(2,1)S(1)}, bf16[128,1024]{1,0:T(8,128)(2,1)S(1)}, bf16[128,1024]{1,0:T(8,128)(2,1)S(1)}, bf16[128,1024]{1,0:T(8,128)(2,1...) custom-call(s32[256]{0:T(256)S(1)} %copy-done.22, ...), custom_call_target="tpu_custom_call" | custom-call | flops 1342177280 | bytes 10485760 | tf_op jit(solution)/shard_map/cond/branch_1_fun/pack/pallas_call | solution.py:303
  109.8 6.5 %collective-permute-done.41.refs_3_ = bf16[128,512]{1,0:T(8,128)(2,1)S(1)} collective-permute-done((bf16[128,512]{1,0:T(8,128)(2,1)S(1)}, bf16[128,512]{1,0:T(8,128)(2,1)S(1)}, u32[]{:S(2)}, u32[]{:S(2)}) %collective-permute-start.41) | collective-permute-done | bytes 131104 | tf_op jit(solution)/shard_map/cond/branch_1_fun/ppermute | solution.py:530
  118.0 11.1 %collective-permute-start.59 = (bf16[128,2048]{1,0:T(8,128)(2,1)S(1)}, bf16[128,2048]{1,0:T(8,128)(2,1)S(1)}, u32[]{:S(2)}, u32[]{:S(2)}) collective-permute-start(bf16[128,2048]{1,0:T(8,128)(2,1)S(1)} %get-tuple-element.160), channel_id=1, source_target_pairs={{0,8},{1,9},{2,10},{3,11},{4,12},{5,13},{6,14},{7,15},{8,0},{9,1},... | collective-permute-start | bytes 1572872 | tf_op jit(solution)/shard_map/cond/branch_1_fun/ppermute | solution.py:530
  135.0 7.2 %contract_chunk.12.refs_14_ = f32[1024,256]{1,0:T(8,128)S(1)} custom-call(s32[256]{0:T(256)S(1)} %copy-done.22, bf16[128,512]{1,0:T(8,128)(2,1)S(1)} %get-tuple-element.165.refs_1_, bf16[128,512]{1,0:T(8,128)(2,1)S(1)} %collective-permute-done.63.refs_2_, bf16[128,512]{1,0:T(8,128)(2,1)S(1)} %collective-permute-done.64.refs_3_, ...), custom_call_target="tpu_custom_call" | custom-call | flops 2415919104 | bytes 12582912 | tf_op jit(solution)/shard_map/cond/branch_1_fun/contract_chunk/pallas_call | solution.py:386
  143.2 48.6 %collective-permute-done.59.refs_5_ = bf16[128,2048]{1,0:T(8,128)(2,1)S(1)} collective-permute-done((bf16[128,2048]{1,0:T(8,128)(2,1)S(1)}, bf16[128,2048]{1,0:T(8,128)(2,1)S(1)}, u32[]{:S(2)}, u32[]{:S(2)}) %collective-permute-start.59) | collective-permute-done | bytes 524320 | tf_op jit(solution)/shard_map/cond/branch_1_fun/ppermute | solution.py:530
  191.8 14.3 %collective-permute-done.60.refs_6_ = bf16[128,2048]{1,0:T(8,128)(2,1)S(1)} collective-permute-done((bf16[128,2048]{1,0:T(8,128)(2,1)S(1)}, bf16[128,2048]{1,0:T(8,128)(2,1)S(1)}, u32[]{:S(2)}, u32[]{:S(2)}) %collective-permute-start.60) | collective-permute-done | bytes 524320 | tf_op jit(solution)/shard_map/cond/branch_1_fun/ppermute | solution.py:530
  206.1 5.0 %collective-permute-start.53 = (bf16[128,1024]{1,0:T(8,128)(2,1)S(1)}, bf16[128,1024]{1,0:T(8,128)(2,1)S(1)}, u32[]{:S(2)}, u32[]{:S(2)}) collective-permute-start(bf16[128,1024]{1,0:T(8,128)(2,1)S(1)} %get-tuple-element.154), channel_id=1, source_target_pairs={{0,12},{1,13},{2,14},{3,15},{4,8},{5,9},{6,10},{7,11},{8,4},{9,5},... | collective-permute-start | bytes 786440 | tf_op jit(solution)/shard_map/cond/branch_1_fun/ppermute | solution.py:530
  211.1 23.2 %contract_chunk.13.refs_14_ = f32[1024,256]{1,0:T(8,128)S(1)} custom-call(s32[256]{0:T(256)S(1)} %copy-done.22, bf16[128,2048]{1,0:T(8,128)(2,1)S(1)} %get-tuple-element.156.refs_1_, bf16[128,2048]{1,0:T(8,128)(2,1)S(1)} %collective-permute-done.56.refs_2_, bf16[128,2048]{1,0:T(8,128)(2,1)S(1)} %collective-permute-done.57.refs_3_, ...), custom_call_target="tpu_custom_call" | custom-call | flops 9663676416 | bytes 25165824 | tf_op jit(solution)/shard_map/cond/branch_1_fun/contract_chunk/pallas_call | solution.py:386
  234.3 31.5 %collective-permute-start.42 = (bf16[128,512]{1,0:T(8,128)(2,1)S(1)}, bf16[128,512]{1,0:T(8,128)(2,1)S(1)}, u32[]{:S(2)}, u32[]{:S(2)}) collective-permute-start(bf16[128,512]{1,0:T(8,128)(2,1)S(1)} %get-tuple-element.139), channel_id=1, source_target_pairs={{0,6},{1,7},{2,4},{3,5},{4,2},{5,3},{6,0},{7,1},{8,14},{9,15},{10,... | collective-permute-start | bytes 393224 | tf_op jit(solution)/shard_map/cond/branch_1_fun/ppermute | solution.py:530
  269.7 3.8 %collective-permute-start.46 = (bf16[128,512]{1,0:T(8,128)(2,1)S(1)}, bf16[128,512]{1,0:T(8,128)(2,1)S(1)}, u32[]{:S(2)}, u32[]{:S(2)}) collective-permute-start(bf16[128,512]{1,0:T(8,128)(2,1)S(1)} %get-tuple-element.143), channel_id=1, source_target_pairs={{0,14},{1,15},{2,12},{3,13},{4,10},{5,11},{6,8},{7,9},{8,6},{9,7},... | collective-permute-start | bytes 393224 | tf_op jit(solution)/shard_map/cond/branch_1_fun/ppermute | solution.py:530
  273.5 13.5 %contract_chunk.14.refs_14_ = f32[1024,256]{1,0:T(8,128)S(1)} custom-call(s32[256]{0:T(256)S(1)} %copy-done.22, bf16[128,1024]{1,0:T(8,128)(2,1)S(1)} %get-tuple-element.148.refs_1_, bf16[128,1024]{1,0:T(8,128)(2,1)S(1)} %collective-permute-done.48.refs_2_, bf16[128,1024]{1,0:T(8,128)(2,1)S(1)} %collective-permute-done.49.refs_3_, ...), custom_call_target="tpu_custom_call" | custom-call | flops 4831838208 | bytes 16777216 | tf_op jit(solution)/shard_map/cond/branch_1_fun/contract_chunk/pallas_call | solution.py:386
  287.1 7.1 %contract_chunk.15.refs_1_ = f32[1024,256]{1,0:T(8,128)S(1)} custom-call(s32[256]{0:T(256)S(1)} %copy-done.22, bf16[128,512]{1,0:T(8,128)(2,1)S(1)} %get-tuple-element.136.refs_1_, bf16[128,512]{1,0:T(8,128)(2,1)S(1)} %collective-permute-done.40.refs_2_, bf16[128,512]{1,0:T(8,128)(2,1)S(1)} %collective-permute-done.41.refs_3_, ...), custom_call_target="tpu_custom_call" | custom-call | flops 2415919104 | bytes 12582912 | tf_op jit(solution)/shard_map/cond/branch_1_fun/contract_chunk/pallas_call | solution.py:386
  295.1 5.9 %split_sums.3 = (f32[8,24,1024]{2,1,0:T(8,128)}, f32[8,24,1024]{2,1,0:T(8,128)}) custom-call(s32[256]{0:T(256)S(1)} %copy-done.22, f32[1024,256]{1,0:T(8,128)} %copy-done.6, s32[1,1024]{1,0:T(1,128)S(1)} %copy-done.39), custom_call_target="tpu_custom_call" | custom-call | bytes 2621440 | tf_op jit(solution)/shard_map/cond/branch_1_fun/split_sums/pallas_call | solution.py:431
  314.1 3.8 %collective-permute-start.77 = (f32[24,1024]{1,0:T(8,128)}, f32[24,1024]{1,0:T(8,128)S(1)}, u32[]{:S(2)}, u32[]{:S(2)}) collective-permute-start(f32[24,1024]{1,0:T(8,128)} %get-tuple-element.182), channel_id=1, source_target_pairs={{0,14},{1,15},{2,12},{3,13},{4,10},{5,11},{6,8},{7,9},{8,6},{9,7},... | collective-permute-start | bytes 294920 | tf_op jit(solution)/shard_map/cond/branch_1_fun/ppermute | solution.py:537
  319.4 4.6 %collective-permute-done.74.refs_8_ = f32[24,1024]{1,0:T(8,128)S(1)} collective-permute-done((f32[24,1024]{1,0:T(8,128)}, f32[24,1024]{1,0:T(8,128)S(1)}, u32[]{:S(2)}, u32[]{:S(2)}) %collective-permute-start.74) | collective-permute-done | bytes 98336 | tf_op jit(solution)/shard_map/cond/branch_1_fun/ppermute | solution.py:537
  (151 shorter events, 64.0 us)
Async XLA Ops:
  41.1 27.9 %collective-permute-start.55 = (bf16[8,64,8192]{2,1,0:T(8,128)(2,1)}, bf16[8,64,8192]{2,1,0:T(8,128)(2,1)}, u32[]{:S(2)}, u32[]{:S(2)}) collective-permute-start(bf16[8,64,8192]{2,1,0:T(8,128)(2,1)} %take_for_sibling.12), channel_id=1, source_target_pairs={{0,1},{1,0},{2,3},{3,2},{4,5},{5,4},{6,7},{7,6},{8,9},{9,8},{10,11... | collective-permute-start | bytes 25165832 | tf_op jit(solution)/shard_map/cond/branch_1_fun/ppermute | solution.py:519
  46.6 49.1 %collective-permute-start.47 = (bf16[8,64,4096]{2,1,0:T(8,128)(2,1)}, bf16[8,64,4096]{2,1,0:T(8,128)(2,1)}, u32[]{:S(2)}, u32[]{:S(2)}) collective-permute-start(bf16[8,64,4096]{2,1,0:T(8,128)(2,1)} %take_for_sibling.11), channel_id=1, source_target_pairs={{0,1},{1,0},{2,3},{3,2},{4,5},{5,4},{6,7},{7,6},{8,9},{9,8},{10,11... | collective-permute-start | bytes 12582920 | tf_op jit(solution)/shard_map/cond/branch_1_fun/ppermute | solution.py:519
  50.5 38.3 %collective-permute-start.39 = (bf16[8,64,2048]{2,1,0:T(8,128)(2,1)}, bf16[8,64,2048]{2,1,0:T(8,128)(2,1)S(1)}, u32[]{:S(2)}, u32[]{:S(2)}) collective-permute-start(bf16[8,64,2048]{2,1,0:T(8,128)(2,1)} %take_for_sibling.10), channel_id=1, source_target_pairs={{0,1},{1,0},{2,3},{3,2},{4,5},{5,4},{6,7},{7,6},{8,9},{9,8},{10,11... | collective-permute-start | bytes 6291464 | tf_op jit(solution)/shard_map/cond/branch_1_fun/ppermute | solution.py:519
  63.7 19.5 %collective-permute-start.65 = (bf16[128,512]{1,0:T(8,128)(2,1)S(1)}, bf16[128,512]{1,0:T(8,128)(2,1)S(1)}, u32[]{:S(2)}, u32[]{:S(2)}) collective-permute-start(bf16[128,512]{1,0:T(8,128)(2,1)S(1)} %get-tuple-element.168), channel_id=1, source_target_pairs={{0,6},{1,7},{2,4},{3,5},{4,2},{5,3},{6,0},{7,1},{8,14},{9,15},{10,... | collective-permute-start | bytes 393224 | tf_op jit(solution)/shard_map/cond/branch_1_fun/ppermute | solution.py:530
  66.4 18.3 %collective-permute-start.66 = (bf16[128,512]{1,0:T(8,128)(2,1)S(1)}, bf16[128,512]{1,0:T(8,128)(2,1)S(1)}, u32[]{:S(2)}, u32[]{:S(2)}) collective-permute-start(bf16[128,512]{1,0:T(8,128)(2,1)S(1)} %get-tuple-element.169), channel_id=1, source_target_pairs={{0,8},{1,9},{2,10},{3,11},{4,12},{5,13},{6,14},{7,15},{8,0},{9,1},... | collective-permute-start | bytes 393224 | tf_op jit(solution)/shard_map/cond/branch_1_fun/ppermute | solution.py:530
  83.2 45.8 %collective-permute-start.56 = (bf16[128,2048]{1,0:T(8,128)(2,1)S(1)}, bf16[128,2048]{1,0:T(8,128)(2,1)S(1)}, u32[]{:S(2)}, u32[]{:S(2)}) collective-permute-start(bf16[128,2048]{1,0:T(8,128)(2,1)S(1)} %get-tuple-element.157), channel_id=1, source_target_pairs={{0,2},{1,3},{2,0},{3,1},{4,6},{5,7},{6,4},{7,5},{8,10},{9,11},{10,... | collective-permute-start | bytes 1572872 | tf_op jit(solution)/shard_map/cond/branch_1_fun/ppermute | solution.py:530
  84.8 46.7 %collective-permute-start.57 = (bf16[128,2048]{1,0:T(8,128)(2,1)S(1)}, bf16[128,2048]{1,0:T(8,128)(2,1)S(1)}, u32[]{:S(2)}, u32[]{:S(2)}) collective-permute-start(bf16[128,2048]{1,0:T(8,128)(2,1)S(1)} %get-tuple-element.158), channel_id=1, source_target_pairs={{0,4},{1,5},{2,6},{3,7},{4,0},{5,1},{6,2},{7,3},{8,12},{9,13},{10,... | collective-permute-start | bytes 1572872 | tf_op jit(solution)/shard_map/cond/branch_1_fun/ppermute | solution.py:530
  85.2 22.1 %collective-permute-start.68 = (bf16[128,512]{1,0:T(8,128)(2,1)S(1)}, bf16[128,512]{1,0:T(8,128)(2,1)S(1)}, u32[]{:S(2)}, u32[]{:S(2)}) collective-permute-start(bf16[128,512]{1,0:T(8,128)(2,1)S(1)} %get-tuple-element.171), channel_id=1, source_target_pairs={{0,12},{1,13},{2,14},{3,15},{4,8},{5,9},{6,10},{7,11},{8,4},{9,5},... | collective-permute-start | bytes 393224 | tf_op jit(solution)/shard_map/cond/branch_1_fun/ppermute | solution.py:530
  88.8 18.9 %collective-permute-start.69 = (bf16[128,512]{1,0:T(8,128)(2,1)S(1)}, bf16[128,512]{1,0:T(8,128)(2,1)S(1)}, u32[]{:S(2)}, u32[]{:S(2)}) collective-permute-start(bf16[128,512]{1,0:T(8,128)(2,1)S(1)} %get-tuple-element.172), channel_id=1, source_target_pairs={{0,14},{1,15},{2,12},{3,13},{4,10},{5,11},{6,8},{7,9},{8,6},{9,7},... | collective-permute-start | bytes 393224 | tf_op jit(solution)/shard_map/cond/branch_1_fun/ppermute | solution.py:530
  107.7 21.3 %collective-permute-start.49 = (bf16[128,1024]{1,0:T(8,128)(2,1)S(1)}, bf16[128,1024]{1,0:T(8,128)(2,1)S(1)}, u32[]{:S(2)}, u32[]{:S(2)}) collective-permute-start(bf16[128,1024]{1,0:T(8,128)(2,1)S(1)} %get-tuple-element.150), channel_id=1, source_target_pairs={{0,4},{1,5},{2,6},{3,7},{4,0},{5,1},{6,2},{7,3},{8,12},{9,13},{10,... | collective-permute-start | bytes 786440 | tf_op jit(solution)/shard_map/cond/branch_1_fun/ppermute | solution.py:530
  116.2 27.0 %collective-permute-start.58 = (bf16[128,2048]{1,0:T(8,128)(2,1)S(1)}, bf16[128,2048]{1,0:T(8,128)(2,1)S(1)}, u32[]{:S(2)}, u32[]{:S(2)}) collective-permute-start(bf16[128,2048]{1,0:T(8,128)(2,1)S(1)} %get-tuple-element.159), channel_id=1, source_target_pairs={{0,6},{1,7},{2,4},{3,5},{4,2},{5,3},{6,0},{7,1},{8,14},{9,15},{10,... | collective-permute-start | bytes 1572872 | tf_op jit(solution)/shard_map/cond/branch_1_fun/ppermute | solution.py:530
  118.0 73.8 %collective-permute-start.59 = (bf16[128,2048]{1,0:T(8,128)(2,1)S(1)}, bf16[128,2048]{1,0:T(8,128)(2,1)S(1)}, u32[]{:S(2)}, u32[]{:S(2)}) collective-permute-start(bf16[128,2048]{1,0:T(8,128)(2,1)S(1)} %get-tuple-element.160), channel_id=1, source_target_pairs={{0,8},{1,9},{2,10},{3,11},{4,12},{5,13},{6,14},{7,15},{8,0},{9,1},... | collective-permute-start | bytes 1572872 | tf_op jit(solution)/shard_map/cond/branch_1_fun/ppermute | solution.py:530
  129.0 77.0 %collective-permute-start.60 = (bf16[128,2048]{1,0:T(8,128)(2,1)S(1)}, bf16[128,2048]{1,0:T(8,128)(2,1)S(1)}, u32[]{:S(2)}, u32[]{:S(2)}) collective-permute-start(bf16[128,2048]{1,0:T(8,128)(2,1)S(1)} %get-tuple-element.161), channel_id=1, source_target_pairs={{0,10},{1,11},{2,8},{3,9},{4,14},{5,15},{6,12},{7,13},{8,2},{9,3},... | collective-permute-start | bytes 1572872 | tf_op jit(solution)/shard_map/cond/branch_1_fun/ppermute | solution.py:530
  129.0 77.0 %collective-permute-start.61 = (bf16[128,2048]{1,0:T(8,128)(2,1)S(1)}, bf16[128,2048]{1,0:T(8,128)(2,1)S(1)}, u32[]{:S(2)}, u32[]{:S(2)}) collective-permute-start(bf16[128,2048]{1,0:T(8,128)(2,1)S(1)} %get-tuple-element.162), channel_id=1, source_target_pairs={{0,12},{1,13},{2,14},{3,15},{4,8},{5,9},{6,10},{7,11},{8,4},{9,5},... | collective-permute-start | bytes 1572872 | tf_op jit(solution)/shard_map/cond/branch_1_fun/ppermute | solution.py:530
  131.4 79.7 %collective-permute-start.62 = (bf16[128,2048]{1,0:T(8,128)(2,1)S(1)}, bf16[128,2048]{1,0:T(8,128)(2,1)S(1)}, u32[]{:S(2)}, u32[]{:S(2)}) collective-permute-start(bf16[128,2048]{1,0:T(8,128)(2,1)S(1)} %get-tuple-element.163), channel_id=1, source_target_pairs={{0,14},{1,15},{2,12},{3,13},{4,10},{5,11},{6,8},{7,9},{8,6},{9,7},... | collective-permute-start | bytes 1572872 | tf_op jit(solution)/shard_map/cond/branch_1_fun/ppermute | solution.py:530
  143.2 91.1 %collective-permute-start.50 = (bf16[128,1024]{1,0:T(8,128)(2,1)S(1)}, bf16[128,1024]{1,0:T(8,128)(2,1)S(1)}, u32[]{:S(2)}, u32[]{:S(2)}) collective-permute-start(bf16[128,1024]{1,0:T(8,128)(2,1)S(1)} %get-tuple-element.151), channel_id=1, source_target_pairs={{0,6},{1,7},{2,4},{3,5},{4,2},{5,3},{6,0},{7,1},{8,14},{9,15},{10,... | collective-permute-start | bytes 786440 | tf_op jit(solution)/shard_map/cond/branch_1_fun/ppermute | solution.py:530
  191.8 74.0 %collective-permute-start.51 = (bf16[128,1024]{1,0:T(8,128)(2,1)S(1)}, bf16[128,1024]{1,0:T(8,128)(2,1)S(1)}, u32[]{:S(2)}, u32[]{:S(2)}) collective-permute-start(bf16[128,1024]{1,0:T(8,128)(2,1)S(1)} %get-tuple-element.152), channel_id=1, source_target_pairs={{0,8},{1,9},{2,10},{3,11},{4,12},{5,13},{6,14},{7,15},{8,0},{9,1},... | collective-permute-start | bytes 786440 | tf_op jit(solution)/shard_map/cond/branch_1_fun/ppermute | solution.py:530
  206.1 59.8 %collective-permute-start.52 = (bf16[128,1024]{1,0:T(8,128)(2,1)S(1)}, bf16[128,1024]{1,0:T(8,128)(2,1)S(1)}, u32[]{:S(2)}, u32[]{:S(2)}) collective-permute-start(bf16[128,1024]{1,0:T(8,128)(2,1)S(1)} %get-tuple-element.153), channel_id=1, source_target_pairs={{0,10},{1,11},{2,8},{3,9},{4,14},{5,15},{6,12},{7,13},{8,2},{9,3},... | collective-permute-start | bytes 786440 | tf_op jit(solution)/shard_map/cond/branch_1_fun/ppermute | solution.py:530
  206.1 62.3 %collective-permute-start.53 = (bf16[128,1024]{1,0:T(8,128)(2,1)S(1)}, bf16[128,1024]{1,0:T(8,128)(2,1)S(1)}, u32[]{:S(2)}, u32[]{:S(2)}) collective-permute-start(bf16[128,1024]{1,0:T(8,128)(2,1)S(1)} %get-tuple-element.154), channel_id=1, source_target_pairs={{0,12},{1,13},{2,14},{3,15},{4,8},{5,9},{6,10},{7,11},{8,4},{9,5},... | collective-permute-start | bytes 786440 | tf_op jit(solution)/shard_map/cond/branch_1_fun/ppermute | solution.py:530
  211.1 58.6 %collective-permute-start.54 = (bf16[128,1024]{1,0:T(8,128)(2,1)S(1)}, bf16[128,1024]{1,0:T(8,128)(2,1)S(1)}, u32[]{:S(2)}, u32[]{:S(2)}) collective-permute-start(bf16[128,1024]{1,0:T(8,128)(2,1)S(1)} %get-tuple-element.155), channel_id=1, source_target_pairs={{0,14},{1,15},{2,12},{3,13},{4,10},{5,11},{6,8},{7,9},{8,6},{9,7},... | collective-permute-start | bytes 786440 | tf_op jit(solution)/shard_map/cond/branch_1_fun/ppermute | solution.py:530
  234.3 52.6 %collective-permute-start.42 = (bf16[128,512]{1,0:T(8,128)(2,1)S(1)}, bf16[128,512]{1,0:T(8,128)(2,1)S(1)}, u32[]{:S(2)}, u32[]{:S(2)}) collective-permute-start(bf16[128,512]{1,0:T(8,128)(2,1)S(1)} %get-tuple-element.139), channel_id=1, source_target_pairs={{0,6},{1,7},{2,4},{3,5},{4,2},{5,3},{6,0},{7,1},{8,14},{9,15},{10,... | collective-permute-start | bytes 393224 | tf_op jit(solution)/shard_map/cond/branch_1_fun/ppermute | solution.py:530
  265.8 21.1 %collective-permute-start.43 = (bf16[128,512]{1,0:T(8,128)(2,1)S(1)}, bf16[128,512]{1,0:T(8,128)(2,1)S(1)}, u32[]{:S(2)}, u32[]{:S(2)}) collective-permute-start(bf16[128,512]{1,0:T(8,128)(2,1)S(1)} %get-tuple-element.140), channel_id=1, source_target_pairs={{0,8},{1,9},{2,10},{3,11},{4,12},{5,13},{6,14},{7,15},{8,0},{9,1},... | collective-permute-start | bytes 393224 | tf_op jit(solution)/shard_map/cond/branch_1_fun/ppermute | solution.py:530
  265.9 21.1 %collective-permute-start.44 = (bf16[128,512]{1,0:T(8,128)(2,1)S(1)}, bf16[128,512]{1,0:T(8,128)(2,1)S(1)}, u32[]{:S(2)}, u32[]{:S(2)}) collective-permute-start(bf16[128,512]{1,0:T(8,128)(2,1)S(1)} %get-tuple-element.141), channel_id=1, source_target_pairs={{0,10},{1,11},{2,8},{3,9},{4,14},{5,15},{6,12},{7,13},{8,2},{9,3},... | collective-permute-start | bytes 393224 | tf_op jit(solution)/shard_map/cond/branch_1_fun/ppermute | solution.py:530
  268.4 18.6 %collective-permute-start.45 = (bf16[128,512]{1,0:T(8,128)(2,1)S(1)}, bf16[128,512]{1,0:T(8,128)(2,1)S(1)}, u32[]{:S(2)}, u32[]{:S(2)}) collective-permute-start(bf16[128,512]{1,0:T(8,128)(2,1)S(1)} %get-tuple-element.142), channel_id=1, source_target_pairs={{0,12},{1,13},{2,14},{3,15},{4,8},{5,9},{6,10},{7,11},{8,4},{9,5},... | collective-permute-start | bytes 393224 | tf_op jit(solution)/shard_map/cond/branch_1_fun/ppermute | solution.py:530
  (45 other events, 461.5 us)
